TPU v7x, 128 devices: a whole 4x4x4 slice. The times are simulated.
128 devices in a mesh: tm: 64 (over z, y, x), blk: 2 (over core).
Axes of the slice: x: 4, y: 4, z: 4, core: 2. Of those that a mesh axis runs over, the one named last changes fastest.
Arguments:
- spatial_factor: bfloat16 [49152, 768], P(('tm', 'blk')), may hold values from -1 to 2
- transition_factor: bfloat16 [49152, 768], P(('tm', 'blk')), may hold values from -3 to 1
- effect_factor: bfloat16 [4096, 768], P(('tm', 'blk')), may hold values from -0.21875 to 0.21875
- node_diag: float32 [49152], P(('tm', 'blk')), may hold values from 0.05 to 0.5
Outputs:
- ends_sys: float32 [64, 2, 768, 1536], P('tm', None, 'blk')
- arrow_sys: float32 [64, 64, 1600], P('tm', 'blk')
- logpivot: float32 [64], P('tm')
All inputs are finite; a program needn't handle non-finite values.
Results may differ from a plain program's by a relative error of at most 0.0003.
Values may be sent and summed in bfloat16 or wider, within the bound.
No kernel may reach another device: no remote copies, remote signals or barrier semaphores. Data moves between devices by JAX's collectives and lax.ppermute only.
A program may use at most 128 MiB of HBM per device.

v0:
```python
import jax
import jax.numpy as jnp
from jax import lax
from jax.sharding import PartitionSpec as P

LEVELS = 3


def passed_along(value, axis, steps):
    count = lax.axis_size(axis)
    initial, last = (max(0, -steps), min(count, count - steps))
    return lax.ppermute(value, axis, [(source, source + steps) for source in range(initial, last)])


def join_segments(lower_seg, upper_seg, node_count, cols_node):
    after = slice(node_count, 2 * node_count)
    first = slice(0, node_count)
    effects = slice(2 * node_count, None)
    own_first = slice(0, cols_node)
    own_after = slice(cols_node, 2 * cols_node)
    own_effects = slice(2 * cols_node, None)
    pivot_part = lower_seg[after, own_after] + upper_seg[first, own_first]
    pivot = lax.all_gather(pivot_part, "blk", axis=1, tiled=True)
    pivot_chol = jnp.linalg.cholesky(pivot)
    coupling = jnp.concatenate(
        [
            lower_seg[after, own_first],
            upper_seg[first, own_after],
            lower_seg[after, own_effects] + upper_seg[first, own_effects],
        ],
        axis=1,
    )
    own_solved = jax.scipy.linalg.solve_triangular(pivot_chol, coupling, lower=True)
    part_first, part_after, part_effects = (
        lax.all_gather(own_solved[:, own_first], "blk", axis=1, tiled=True),
        lax.all_gather(own_solved[:, own_after], "blk", axis=1, tiled=True),
        lax.all_gather(own_solved[:, own_effects], "blk", axis=1, tiled=True),
    )
    solved = jnp.concatenate([part_first, part_after, part_effects], axis=1)
    blank = jnp.zeros((node_count, cols_node), jnp.float32)
    col_first = jnp.concatenate(
        [lower_seg[first, own_first], blank, lower_seg[effects, own_first]], axis=0
    )
    col_after = jnp.concatenate(
        [blank, upper_seg[after, own_after], upper_seg[effects, own_after]], axis=0
    )
    col_effects = jnp.concatenate(
        [
            lower_seg[first, own_effects],
            upper_seg[after, own_effects],
            lower_seg[effects, own_effects] + upper_seg[effects, own_effects],
        ],
        axis=0,
    )
    retained = jnp.concatenate([col_first, col_after, col_effects], axis=1)
    correction = lax.dot_general(
        solved,
        own_solved,
        (((0,), (0,)), ((), ())),
        precision=lax.Precision.HIGHEST,
        preferred_element_type=jnp.float32,
    )
    step_logs = 2.0 * jnp.sum(jnp.log(jnp.diag(pivot_chol)))
    return (retained - correction, step_logs)


def shards(spatial_factor, transition_factor, effect_factor, node_diag):
    cols_node = spatial_factor.shape[0]
    node_count = spatial_factor.shape[1]
    spatial_all, transition_all, effect_all = (
        lax.all_gather(spatial_factor, "blk", axis=0, tiled=True),
        lax.all_gather(transition_factor, "blk", axis=0, tiled=True),
        lax.all_gather(effect_factor, "blk", axis=0, tiled=True),
    )
    stacked = jnp.concatenate([spatial_all, transition_all, effect_all], axis=0)
    own_rows = jnp.concatenate([spatial_factor, transition_factor, effect_factor], axis=0)
    system = lax.dot_general(
        stacked, own_rows, (((1,), (1,)), ((), ())), preferred_element_type=jnp.float32
    )
    row_ids = lax.broadcasted_iota(jnp.int32, (stacked.shape[0], cols_node), 0)
    col_ids = lax.broadcasted_iota(jnp.int32, (stacked.shape[0], cols_node), 1)
    target = lax.axis_index("blk") * cols_node + col_ids
    diag_cols = jnp.where(row_ids == target, node_diag[None, :], jnp.zeros((), jnp.float32))
    system = jnp.concatenate([system[:, :cols_node] + diag_cols, system[:, cols_node:]], axis=1)
    logs = jnp.zeros((), jnp.float32)
    tm_index = lax.axis_index("tm")
    for level_index in range(LEVELS):
        partner, partner_logs = passed_along((system, logs), "tm", -(2**level_index))
        joined, step_logs = join_segments(system, partner, node_count, cols_node)
        keeps_sum = tm_index % 2 ** (level_index + 1) == 0
        system = jnp.where(keeps_sum, joined, system)
        logs = jnp.where(keeps_sum, logs + partner_logs + step_logs, logs)
    for level_index in reversed(range(LEVELS)):
        received, received_logs = passed_along((system, logs), "tm", 2**level_index)
        takes_copy = tm_index % 2 ** (level_index + 1) == 2**level_index
        system = jnp.where(takes_copy, received, system)
        logs = jnp.where(takes_copy, received_logs, logs)
    flipped = system.T
    ends_sys = jnp.stack(
        [
            flipped[:cols_node, : 2 * node_count],
            flipped[cols_node : 2 * cols_node, : 2 * node_count],
        ],
        axis=0,
    )[None]
    arrow_sys = flipped[2 * cols_node :, :][None]
    logpivot = (logs / ((2**LEVELS - 1) * node_count)).reshape(1)
    return (ends_sys, arrow_sys, logpivot)


def solution(mesh):
    return jax.shard_map(
        shards,
        mesh=mesh,
        in_specs=(
            P(("tm", "blk"), None),
            P(("tm", "blk"), None),
            P(("tm", "blk"), None),
            P(("tm", "blk")),
        ),
        out_specs=(P("tm", None, "blk", None), P("tm", "blk", None), P("tm")),
        check_vma=False,
    )
```

profile of v0, /device:TPU:32, one launch (start us, length us, event | category | flops | bytes accessed | tf_op | source)
XLA Modules:
  0.0 1813.6 jit_solution(12091078845445352355)
XLA Ops:
  10.8 12.9 all-gather.12.cloned.1.call-done
  23.7 14.9 all-gather.14.cloned.1.call-done
  52.8 114.5 %collective-permute-done = f32[1600,800]{0,1:T(8,128)S(1)} collective-permute-done((f32[1600,800]{0,1:T(8,128)S(1)}, f32[1600,800]{0,1:T(8,128)S(1)}, u32[]{:S(2)}, u32[]{:S(2)}) %collective-permute-start) | collective-permute-done | bytes 5120032 | tf_op jit(solution)/shard_map/ppermute | solution.py:12
  174.4 12.5 all-gather.16.cloned.1.call-done
  271.9 12.2 cholesky.650
  344.9 17.6 while.6
  362.5 59.0 %custom-call.58 = f32[6,128,128]{1,2,0:T(8,128)S(1)} custom-call(f32[6,128,128]{2,1,0:T(8,128)S(1)} %get-tuple-element.25), custom_call_target="InvertDiagBlocksLowerTriangular" | custom-call | tf_op jit(solution)/shard_map/jit(_solve_triangular)/triangular_solve | solution.py:33
  453.3 16.5 all-gather.20.cloned.1.call-done
  471.0 22.8 %fusion.4 = f32[1600,800]{0,1:T(8,128)} fusion(f32[768,384]{0,1:T(8,128)} %broadcast.216, f32[832,384]{0,1:T(8,128)} %slice.373, f32[64,32]{0,1:T(8,128)S(1)} %slice_add_fusion.9, f32[768,32]{0,1:T(8,128)S(1)} %get-tuple-element.84, f32[768,32]{0,1:T(8,128)S(1)} %get-tuple-element.83, f32[64,384]{0,1:T(8,128)S(1)} %slice-done, ...), kind=kOutput, calls=%fused_computation.18 | convolution fusion | flops 11815577600 | bytes 21553152 | tf_op jit(solution)/shard_map/dot_general | solution.py:56
  500.8 114.8 %collective-permute-done.1 = f32[1600,800]{0,1:T(8,128)S(1)} collective-permute-done((f32[1600,800]{0,1:T(8,128)}, f32[1600,800]{0,1:T(8,128)S(1)}, u32[]{:S(2)}, u32[]{:S(2)}) %collective-permute-start.1) | collective-permute-done | bytes 5120032 | tf_op jit(solution)/shard_map/ppermute | solution.py:12
  624.2 14.0 all-gather.22.cloned.1.call-done
  785.9 17.7 while.7
  803.6 59.0 %custom-call.64 = f32[6,128,128]{1,2,0:T(8,128)S(1)} custom-call(f32[6,128,128]{2,1,0:T(8,128)S(1)} %get-tuple-element.26), custom_call_target="InvertDiagBlocksLowerTriangular" | custom-call | tf_op jit(solution)/shard_map/jit(_solve_triangular)/triangular_solve | solution.py:33
  894.2 16.7 all-gather.26.cloned.1.call-done
  910.9 22.0 %fusion.9 = f32[1600,800]{0,1:T(8,128)} fusion(f32[1600,800]{0,1:T(8,128)} %fusion.4, f32[768,384]{0,1:T(8,128)} %broadcast.216, f32[832,384]{0,1:T(8,128)} %slice.389, f32[64,32]{0,1:T(8,128)S(1)} %slice_add_fusion.8, f32[768,32]{0,1:T(8,128)S(1)} %get-tuple-element.79, f32[768,32]{0,1:T(8,128)S(1)} %get-tuple-element.78, f32[64,384]{0,1:T(8,128)S(1)} %slice.388, ...), kind=kOutput, calls=%fused_computation.23 | convolution fusion | flops 11814297600 | bytes 21553152 | tf_op jit(solution)/shard_map/dot_general | solution.py:56
  937.5 114.8 %collective-permute-done.2 = f32[1600,800]{0,1:T(8,128)S(1)} collective-permute-done((f32[1600,800]{0,1:T(8,128)}, f32[1600,800]{0,1:T(8,128)S(1)}, u32[]{:S(2)}, u32[]{:S(2)}) %collective-permute-start.2) | collective-permute-done | bytes 5120032 | tf_op jit(solution)/shard_map/ppermute | solution.py:12
  1060.9 14.5 all-gather.28.cloned.1.call-done
  1222.8 17.7 while.8
  1240.6 59.0 %custom-call.70 = f32[6,128,128]{1,2,0:T(8,128)S(1)} custom-call(f32[6,128,128]{2,1,0:T(8,128)S(1)} %get-tuple-element.27), custom_call_target="InvertDiagBlocksLowerTriangular" | custom-call | tf_op jit(solution)/shard_map/jit(_solve_triangular)/triangular_solve | solution.py:33
  1331.2 16.7 all-gather.32.cloned.1.call-done
  1347.9 22.0 %fusion.14 = f32[1600,800]{0,1:T(8,128)} fusion(f32[1600,800]{0,1:T(8,128)} %fusion.9, f32[768,384]{0,1:T(8,128)} %broadcast.216, f32[832,384]{0,1:T(8,128)} %slice.405, f32[64,32]{0,1:T(8,128)S(1)} %slice_add_fusion.7, f32[768,32]{0,1:T(8,128)S(1)} %get-tuple-element.72, f32[768,32]{0,1:T(8,128)S(1)} %get-tuple-element.71, f32[64,384]{0,1:T(8,128)S(1)} %slice.404, ...), kind=kOutput, calls=%fused_computation.28 | convolution fusion | flops 11814297600 | bytes 21553152 | tf_op jit(solution)/shard_map/dot_general | solution.py:56
  1373.8 117.4 %collective-permute-done.3 = f32[1600,800]{0,1:T(8,128)} collective-permute-done((f32[1600,800]{0,1:T(8,128)}, f32[1600,800]{0,1:T(8,128)}, u32[]{:S(2)}, u32[]{:S(2)}) %collective-permute-start.3) | collective-permute-done | bytes 5120032 | tf_op jit(solution)/shard_map/ppermute | solution.py:12
  1502.0 117.5 %collective-permute-done.4 = f32[1600,800]{0,1:T(8,128)} collective-permute-done((f32[1600,800]{0,1:T(8,128)}, f32[1600,800]{0,1:T(8,128)}, u32[]{:S(2)}, u32[]{:S(2)}) %collective-permute-start.4) | collective-permute-done | bytes 5120032 | tf_op jit(solution)/shard_map/ppermute | solution.py:12
  1644.7 97.3 %collective-permute-start.7 = (f32[]{:T(128)}, f32[]{:T(128)}, u32[]{:S(2)}, u32[]{:S(2)}) collective-permute-start(f32[]{:T(128)} %select_n.111), channel_id=1, source_target_pairs={{4,0},{6,2},{8,4},{10,6},{12,8},{14,10},{16,12},{18,14},{20,16},{2... | collective-permute-start | bytes 20 | tf_op jit(solution)/shard_map/ppermute | solution.py:12
  (356 shorter events, 728.8 us)
Async XLA Ops:
  7.2 16.5 all-gather.12.cloned.1.call-start
  7.9 30.8 %all-gather.14.cloned.1.call-start = ((), (), s32[]{:S(2)}) async-start(), calls=%async_computation.1 | async-start | bytes 1769472 | tf_op jit(solution)/shard_map/all_gather | solution.py:72
  8.6 178.3 %all-gather.16.cloned.1.call-start = ((), (), s32[]{:S(2)}) async-start(), calls=%async_computation.2 | async-start | bytes 3538944 | tf_op jit(solution)/shard_map/all_gather | solution.py:23
  45.7 393.1 %copy-start = (f32[1600,384]{0,1:T(8,128)}, f32[1600,384]{0,1:T(8,128)S(1)}, u32[]{:S(2)}) copy-start(f32[1600,384]{0,1:T(8,128)S(1)} %slice_add_fusion) | copy-start | bytes 7372804
  46.1 121.2 %collective-permute-start = (f32[1600,800]{0,1:T(8,128)S(1)}, f32[1600,800]{0,1:T(8,128)S(1)}, u32[]{:S(2)}, u32[]{:S(2)}) collective-permute-start(f32[1600,800]{0,1:T(8,128)S(1)} %pad_maximum_fusion.3), channel_id=1, source_target_pairs={{2,0},{4,2},{6,4},{8,6},{10,8},{12,10},{14,12},{16,14},{18,16},{20... | collective-permute-start | bytes 15360008 | tf_op jit(solution)/shard_map/ppermute | solution.py:12
  170.4 282.9 %all-gather.18.cloned.1.call-start = ((), (), s32[]{:S(2)}) async-start(), calls=%async_computation.3 | async-start | bytes 3538944 | tf_op jit(solution)/shard_map/all_gather | solution.py:35
  438.2 31.7 %all-gather.20.cloned.1.call-start = ((), (), s32[]{:S(2)}) async-start(), calls=%async_computation.4 | async-start | bytes 3538944 | tf_op jit(solution)/shard_map/all_gather | solution.py:36
  438.8 199.4 %all-gather.22.cloned.1.call-start = ((), (), s32[]{:S(2)}) async-start(), calls=%async_computation.5 | async-start | bytes 3538944 | tf_op jit(solution)/shard_map/all_gather | solution.py:23
  493.8 121.8 %collective-permute-start.1 = (f32[1600,800]{0,1:T(8,128)}, f32[1600,800]{0,1:T(8,128)S(1)}, u32[]{:S(2)}, u32[]{:S(2)}) collective-permute-start(f32[1600,800]{0,1:T(8,128)} %fusion.4), channel_id=1, source_target_pairs={{4,0},{6,2},{8,4},{10,6},{12,8},{14,10},{16,12},{18,14},{20,16},{2... | collective-permute-start | bytes 15360008 | tf_op jit(solution)/shard_map/ppermute | solution.py:12
  621.5 272.7 %all-gather.24.cloned.1.call-start = ((), (), s32[]{:S(2)}) async-start(), calls=%async_computation.6 | async-start | bytes 3538944 | tf_op jit(solution)/shard_map/all_gather | solution.py:35
  879.1 31.8 %all-gather.26.cloned.1.call-start = ((), (), s32[]{:S(2)}) async-start(), calls=%async_computation.7 | async-start | bytes 3538944 | tf_op jit(solution)/shard_map/all_gather | solution.py:36
  879.8 195.6 %all-gather.28.cloned.1.call-start = ((), (), s32[]{:S(2)}) async-start(), calls=%async_computation.8 | async-start | bytes 3538944 | tf_op jit(solution)/shard_map/all_gather | solution.py:23
  932.9 119.4 %collective-permute-start.2 = (f32[1600,800]{0,1:T(8,128)}, f32[1600,800]{0,1:T(8,128)S(1)}, u32[]{:S(2)}, u32[]{:S(2)}) collective-permute-start(f32[1600,800]{0,1:T(8,128)} %fusion.9), channel_id=1, source_target_pairs={{8,0},{10,2},{12,4},{14,6},{16,8},{18,10},{20,12},{22,14},{24,16},... | collective-permute-start | bytes 15360008 | tf_op jit(solution)/shard_map/ppermute | solution.py:12
  1058.2 273.0 %all-gather.30.cloned.1.call-start = ((), (), s32[]{:S(2)}) async-start(), calls=%async_computation.9 | async-start | bytes 3538944 | tf_op jit(solution)/shard_map/all_gather | solution.py:35
  1316.1 31.8 %all-gather.32.cloned.1.call-start = ((), (), s32[]{:S(2)}) async-start(), calls=%async_computation.10 | async-start | bytes 3538944 | tf_op jit(solution)/shard_map/all_gather | solution.py:36
  1369.9 121.3 %collective-permute-start.3 = (f32[1600,800]{0,1:T(8,128)}, f32[1600,800]{0,1:T(8,128)}, u32[]{:S(2)}, u32[]{:S(2)}) collective-permute-start(f32[1600,800]{0,1:T(8,128)} %fusion.14), channel_id=1, source_target_pairs={{0,8},{2,10},{4,12},{6,14},{8,16},{10,18},{12,20},{14,22},{16,24},... | collective-permute-start | bytes 15360008 | tf_op jit(solution)/shard_map/ppermute | solution.py:12
  1496.6 122.9 %collective-permute-start.4 = (f32[1600,800]{0,1:T(8,128)}, f32[1600,800]{0,1:T(8,128)}, u32[]{:S(2)}, u32[]{:S(2)}) collective-permute-start(f32[1600,800]{0,1:T(8,128)} %broadcast_select_fusion), channel_id=1, source_target_pairs={{0,4},{2,6},{4,8},{6,10},{8,12},{10,14},{12,16},{14,18},{16,20},{1... | collective-permute-start | bytes 15360008 | tf_op jit(solution)/shard_map/ppermute | solution.py:12
  1625.0 173.8 %collective-permute-start.5 = (f32[1600,800]{0,1:T(8,128)}, f32[1600,800]{0,1:T(8,128)}, u32[]{:S(2)}, u32[]{:S(2)}) collective-permute-start(f32[1600,800]{0,1:T(8,128)} %broadcast_select_fusion.1), channel_id=1, source_target_pairs={{0,2},{2,4},{4,6},{6,8},{8,10},{10,12},{12,14},{14,16},{16,18},{18... | collective-permute-start | bytes 15360008 | tf_op jit(solution)/shard_map/ppermute | solution.py:12
  1628.9 15.2 collective-permute-start.6
  1644.7 97.3 %collective-permute-start.7 = (f32[]{:T(128)}, f32[]{:T(128)}, u32[]{:S(2)}, u32[]{:S(2)}) collective-permute-start(f32[]{:T(128)} %select_n.111), channel_id=1, source_target_pairs={{4,0},{6,2},{8,4},{10,6},{12,8},{14,10},{16,12},{18,14},{20,16},{2... | collective-permute-start | bytes 20 | tf_op jit(solution)/shard_map/ppermute | solution.py:12
  1756.0 5.4 collective-permute-start.8
  1769.6 7.5 collective-permute-start.9
  1777.8 10.2 collective-permute-start.10
  1788.6 9.6 collective-permute-start.11
  (24 other events, 534.8 us)
Sparse Core Ops, SparseCore 0:
  9.6 14.0 all-gather.11
  25.3 13.2 all-gather.13
  170.5 16.3 all-gather.15
  438.3 14.9 all-gather.17
  454.8 14.9 all-gather.19
  621.6 16.5 all-gather.21
  879.2 14.9 all-gather.23
  895.9 14.9 all-gather.25
  1058.3 17.0 all-gather.27
  1316.2 14.9 all-gather.29
  1332.9 14.9 all-gather.31
where the time goes:
time: 1820 us; the launch traced here: 1810 us
  waiting for transfers between devices  739 us (41%)
  other arithmetic  610 us (34%)
  starting transfers between devices  156 us (9%)
  matrix products  148 us (8%)
  local copies, waits for them, and re-layouts  119 us (7%)
  between operations  33.5 us (2%)
    ppermute x12, waiting for transfers between devices, passed_along(): lax.ppermute(value, axis, [(source, source + steps) for source in range(i...  593 us
    another operation x68, other arithmetic, join_segments(): pivot_chol = jnp.linalg.cholesky(pivot)  375 us
    another operation x7, other arithmetic, join_segments(): jax.scipy.linalg.solve_triangular(pivot_chol, coupling, lower=True)  186 us
    ppermute x12, starting transfers between devices, passed_along(): lax.ppermute(value, axis, [(source, source + steps) for source in range(i...  155 us
    dot_general x3, matrix products, join_segments(): lax.dot_general(solved, own_solved, (((0,), (0,)), ((), ())), precision=l...  66.8 us
    another operation x58, local copies, waits for them, and re-layouts, join_segments(): jax.scipy.linalg.solve_triangular(pivot_chol, coupling, lower=True)  52.8 us
    all_gather x3, waiting for transfers between devices, join_segments(): lax.all_gather(own_solved[:, own_after], 'blk', axis=1, tiled=True)  49.9 us
    another operation x33, matrix products, join_segments(): jax.scipy.linalg.solve_triangular(pivot_chol, coupling, lower=True)  42.7 us
  transfers between devices with their start and end apart: 23, of which 20 were waited for; matrix products, arithmetic and copies ran while one was open for 3% of the time, Pallas kernels for 0%

commit v1 on v0

v1 whole, which is shorter than its diff:
```python
import functools

import jax
import jax.numpy as jnp
from jax import lax
from jax.experimental import pallas as pl
from jax.experimental.pallas import tpu as pltpu
from jax.sharding import PartitionSpec as P

F32 = jnp.float32
BF16 = jnp.bfloat16
TILE = 8
LANES = 128


def split(x):
    high = x.astype(BF16)
    return high, (x - high.astype(F32)).astype(BF16)


def dot3(a, b):
    dot = functools.partial(jnp.dot, preferred_element_type=F32)
    return dot(a[0], b[0]) + (dot(a[0], b[1]) + dot(a[1], b[0]))


def rows8(v, q):
    return jnp.broadcast_to(v[q : q + 1, :], (TILE, LANES))


def lane8(v, j):
    return jnp.broadcast_to(v[:, j : j + 1], (TILE, LANES))


def invert8(cols):
    sub = lax.broadcasted_iota(jnp.int32, (TILE, LANES), 0)
    pivots = []
    for q in range(TILE):
        here = sub == q
        row = [rows8(cols[j], q) for j in range(TILE)]
        pivots.append(row[q][0:1])
        inv = pltpu.reciprocal(row[q], approx=True)
        inv = inv * (2.0 - row[q] * inv)
        new = []
        for j in range(TILE):
            if j == q:
                new.append(jnp.where(here, inv, -cols[q] * inv))
            else:
                scaled = row[j] * inv
                new.append(jnp.where(here, scaled, cols[j] - cols[q] * scaled))
        cols = new
    return cols, pivots


def invert128(tiles):
    lane = lax.broadcasted_iota(jnp.int32, (TILE, LANES), 1)
    sub = lax.broadcasted_iota(jnp.int32, (TILE, LANES), 0)
    logs = jnp.zeros((1, LANES), F32)
    for p in range(LANES // TILE):
        inside = (lane >= TILE * p) & (lane < TILE * p + TILE)
        own = tiles[p]
        inverse, pivots = invert8([lane8(own, TILE * p + j) for j in range(TILE)])
        for pivot in pivots:
            logs = logs + jnp.log(pivot)
        own = jnp.where(inside, (lane - TILE * p == sub).astype(F32), own)
        parts = [inverse[j] * rows8(own, j) for j in range(TILE)]
        solved = ((parts[0] + parts[1]) + (parts[2] + parts[3])) + (
            (parts[4] + parts[5]) + (parts[6] + parts[7])
        )
        spread = [rows8(solved, j) for j in range(TILE)]
        new = []
        for i in range(LANES // TILE):
            if i == p:
                new.append(solved)
                continue
            parts = [lane8(tiles[i], TILE * p + j) * spread[j] for j in range(TILE)]
            total = ((parts[0] + parts[1]) + (parts[2] + parts[3])) + (
                (parts[4] + parts[5]) + (parts[6] + parts[7])
            )
            new.append(jnp.where(inside, 0.0, tiles[i]) - total)
        tiles = new
    return tiles, logs


def inverse_kernel(m_ref, o_ref, l_ref):
    size = m_ref.shape[0]
    o_ref[...] = m_ref[...]

    def body(k, logs):
        ks = pl.ds(pl.multiple_of(k * LANES, LANES), LANES)
        tiles = [
            o_ref[pl.ds(pl.multiple_of(k * LANES + TILE * i, TILE), TILE), ks]
            for i in range(LANES // TILE)
        ]
        tiles, more = invert128(tiles)
        block = jnp.concatenate(tiles, 0)
        block_parts = split(block)
        col = split(o_ref[:, ks])
        solved = dot3(block_parts, split(o_ref[ks, :]))
        update = dot3(col, split(solved))
        left = dot3(col, block_parts)
        o_ref[...] = o_ref[...] - update
        o_ref[:, ks] = -left
        o_ref[ks, :] = solved
        o_ref[ks, ks] = block
        return logs + more

    logs = lax.fori_loop(0, size // LANES, body, jnp.zeros((1, LANES), F32))
    l_ref[...] = jnp.broadcast_to(logs, (TILE, LANES))


def inverse(m):
    size = m.shape[0]
    vmem = pl.BlockSpec(memory_space=pltpu.VMEM)
    return pl.pallas_call(
        inverse_kernel,
        out_shape=(
            jax.ShapeDtypeStruct((size, size), F32),
            jax.ShapeDtypeStruct((TILE, LANES), F32),
        ),
        in_specs=[vmem],
        out_specs=(vmem, vmem),
        compiler_params=pltpu.CompilerParams(vmem_limit_bytes=40 << 20),
        cost_estimate=pl.CostEstimate(
            flops=30_000_000_000, bytes_accessed=8 * size * size, transcendentals=size
        ),
        name="inverse",
    )(m)


def high(a, b):
    return lax.dot_general(
        a,
        b,
        (((0,), (0,)), ((), ())),
        precision=lax.Precision.HIGH,
        preferred_element_type=F32,
    )


def outer(a, b):
    return lax.dot_general(a, b, (((1,), (1,)), ((), ())), preferred_element_type=F32)


def shards(spatial, transition, effect, diag):
    half = spatial.shape[0]
    nodes = 2 * half
    steps = lax.axis_size("tm")
    index = lax.axis_index("tm")
    core = lax.axis_index("blk")
    bit = [(index // 2**r) % 2 for r in range(3)]

    def other_core(x):
        return lax.ppermute(x, "blk", [(0, 1), (1, 0)])

    def partner(x, level):
        if level == 1:
            pairs = [(t, (t // 4) * 4 + 3 - t % 4) for t in range(steps)]
        else:
            pairs = [(t, t ^ (1, 2, 4)[level]) for t in range(steps)]
        return lax.ppermute(x, "tm", pairs)

    def both(x):
        return jnp.concatenate([x, other_core(x)], axis=0)

    def turned(x):
        mid = x.shape[0] // 2
        return jnp.concatenate([x[mid:], x[:mid]], axis=0)

    def join(inv, x1, x2, xk, w1, w2, wk1, wk2, wkk, last):
        own = jnp.concatenate([x1, x2, xk], axis=1)
        far = turned(other_core(own))
        c1, c2, ck = high(inv, x1), high(inv, x2), high(inv, xk)
        f1 = jnp.concatenate([x1, far[:, :half]], axis=1)
        f2 = jnp.concatenate([x2, far[:, half:nodes]], axis=1)
        fk = jnp.concatenate([xk, far[:, nodes:]], axis=1)
        if last:
            flip = core == 1
            f1 = jnp.where(flip, jnp.concatenate([far[:, :half], x1], axis=1), f1)
            f2 = jnp.where(flip, jnp.concatenate([far[:, half:nodes], x2], axis=1), f2)
            fk = jnp.where(flip, jnp.concatenate([far[:, nodes:], xk], axis=1), fk)
            w1, w2, wk1, wk2, wkk = [
                jnp.where(flip, turned(w), w).T for w in (w1, w2, wk1, wk2, wkk)
            ]
            return (
                jnp.concatenate([w1 - high(c1, f1), -high(c1, f2)], axis=1),
                jnp.concatenate([-high(c2, f1), w2 - high(c2, f2)], axis=1),
                jnp.concatenate(
                    [wk1 - high(ck, f1), wk2 - high(ck, f2), wkk - high(ck, fk)], axis=1
                ),
            )
        return (
            w1 - high(f1, c1),
            -high(f1, c2),
            wk1 - high(f1, ck),
            w2 - high(f2, c2),
            wk2 - high(f2, ck),
            wkk - high(fk, ck),
        )

    lower = bit[0] == 0
    pivot_own = jnp.where(lower, transition, spatial)
    keep_own = jnp.where(lower, spatial, transition)
    pivot_got = partner(pivot_own, 0)
    diag_got = partner(diag, 0)
    keep_got = partner(keep_own, 0)
    effect_got = partner(effect, 0)
    p_own, p_got = both(pivot_own), both(pivot_got)
    pivot_diag = both(jnp.where(lower, diag_got, diag))
    stacked = jnp.concatenate([p_own, p_got], axis=1)
    ids = lax.broadcasted_iota(jnp.int32, (nodes, nodes), 0)
    eye = ids == lax.broadcasted_iota(jnp.int32, (nodes, nodes), 1)
    m = outer(stacked, stacked) + jnp.where(eye, pivot_diag[None, :], 0.0)
    inv, logs = inverse(m)
    mine = bit[0] != bit[1]
    p1, p2 = jnp.where(mine, p_own, p_got), jnp.where(mine, p_got, p_own)
    k1, k2 = jnp.where(mine, keep_own, keep_got), jnp.where(mine, keep_got, keep_own)
    e1, e2 = jnp.where(mine, effect, effect_got), jnp.where(mine, effect_got, effect)
    keep_diag = jnp.where(lower, diag, diag_got)
    after = bit[1] == 1
    s1, s2 = both(k1), both(k2)
    eye_half = eye[:, :half]
    w1 = outer(s1, k1) + jnp.where(eye_half & after, keep_diag[None, :], 0.0)
    w2 = outer(s2, k2) + jnp.where(eye_half & ~after, keep_diag[None, :], 0.0)
    ef1, ef2 = both(e1), both(e2)
    ee, er, ek, rr, rk, kk = join(
        inv,
        outer(p1, k1),
        outer(p2, k2),
        outer(p1, e1) + outer(p2, e2),
        w1,
        w2,
        outer(s1, e1),
        outer(s2, e2),
        outer(ef1, e1) + outer(ef2, e2),
        False,
    )
    total = jnp.sum(logs[0:1, 0:1])
    for level in (1, 2):
        last = level == 2
        m_own = ee + partner(ee, level)
        coupling = jnp.concatenate([er, ek], axis=1)
        coupling_got = partner(coupling, level)
        rr_got = partner(rr, level)
        small = jnp.concatenate([rk, kk], axis=0)
        small_got = partner(small, level)
        total_got = partner(total, level)
        m = jnp.concatenate([m_own, turned(other_core(m_own))], axis=1)
        inv, logs = inverse(m)
        mine = bit[2] == 0 if last else bit[1] != bit[2]
        er_got, ek_got = coupling_got[:, :half], coupling_got[:, half:]
        rk_got, kk_got = small_got[:nodes], small_got[nodes:]
        result = join(
            inv,
            jnp.where(mine, er, er_got),
            jnp.where(mine, er_got, er),
            ek + ek_got,
            jnp.where(mine, rr, rr_got),
            jnp.where(mine, rr_got, rr),
            jnp.where(mine, rk, rk_got),
            jnp.where(mine, rk_got, rk),
            kk + kk_got,
            last,
        )
        total = total + total_got + jnp.sum(logs[0:1, 0:1])
        if not last:
            ee, er, ek, rr, rk, kk = result
    ends = jnp.stack([result[0], result[1]], axis=0)[None]
    return ends, result[2][None], (total / (7 * nodes)).reshape(1)


def solution(mesh):
    return jax.shard_map(
        shards,
        mesh=mesh,
        in_specs=(
            P(("tm", "blk"), None),
            P(("tm", "blk"), None),
            P(("tm", "blk"), None),
            P(("tm", "blk")),
        ),
        out_specs=(P("tm", None, "blk", None), P("tm", "blk", None), P("tm")),
        check_vma=False,
    )
```

time: 1820 us -> 432 us (0.24)
  waiting for transfers between devices: 739 us -> 107 us
  other arithmetic: 610 us -> 33.2 us
  starting transfers between devices: 156 us -> 23.3 us
  Pallas kernels: 0 us -> 104 us
  local copies, waits for them, and re-layouts: 119 us -> 54.9 us
  matrix products: 148 us -> 96.3 us
  between operations: 33.5 us -> 6.12 us
    another operation x75 -> x2, other arithmetic: 561 us -> 0.31 us  [shards(): ends = jnp.stack([result[0], result[1]], axis=0)[None]]
    ppermute x12 -> x26, waiting for transfers between devices: 593 us -> 107 us  [the longest x14 106 us: partner(): return lax.ppermute(x, 'tm', pairs)]
    all_gather x11 -> x0, waiting for transfers between devices: 143 us -> none  [the longest x3 49.9 us: join_segments(): lax.all_gather(own_solved[:, own_after], 'blk', axis=1, tiled=True)]
    ppermute x12 -> x26, starting transfers between devices: 155 us -> 23.3 us  [the longest x14 21.5 us: partner(): return lax.ppermute(x, 'tm', pairs)]
    pallas_call x0 -> x3, Pallas kernels: none -> 104 us  [inverse(): pl.pallas_call(inverse_kernel, out_shape=(jax.ShapeDtypeStruct((size, siz...]
    another operation x63 -> x0, matrix products: 76.7 us -> none  [the longest x33 42.7 us: join_segments(): jax.scipy.linalg.solve_triangular(pivot_chol, coupling, lower=True)]
    another operation x78 -> x0, local copies, waits for them, and re-layouts: 56.5 us -> none  [the longest x58 52.8 us: join_segments(): jax.scipy.linalg.solve_triangular(pivot_chol, coupling, lower=True)]
    dot_general x4 -> x39, matrix products: 71.2 us -> 96.3 us  [the longest x28 77 us: high(): lax.dot_general(a, b, (((0,), (0,)), ((), ())), precision=lax.Precision.H...]
  transfers between devices with their start and end apart: 23 -> 26, of which waited for: 20 -> 8; matrix products, arithmetic and copies ran while one was open for 3% -> 31% of each run, Pallas kernels for 0% -> 24%
where the time goes in v1:
time: 432 us; the launch traced here: 425 us
  waiting for transfers between devices  107 us (25%)
  Pallas kernels  104 us (24%)
  matrix products  96.3 us (22%)
  local copies, waits for them, and re-layouts  54.9 us (13%)
  other arithmetic  33.2 us (8%)
  starting transfers between devices  23.3 us (5%)
  between operations  6.12 us (1%)
    ppermute x14, waiting for transfers between devices, partner(): return lax.ppermute(x, 'tm', pairs)  106 us
    pallas_call x3, Pallas kernels, inverse(): pl.pallas_call(inverse_kernel, out_shape=(jax.ShapeDtypeStruct((size, siz...  104 us
    dot_general x28, matrix products, high(): lax.dot_general(a, b, (((0,), (0,)), ((), ())), precision=lax.Precision.H...  77 us
    unnamed x144, local copies, waits for them, and re-layouts  24.7 us
    ppermute x14, starting transfers between devices, partner(): return lax.ppermute(x, 'tm', pairs)  21.5 us
    dot_general x11, matrix products, outer(): lax.dot_general(a, b, (((1,), (1,)), ((), ())), preferred_element_type=F32)  19.3 us
    slice x8, local copies, waits for them, and re-layouts, turned(): return jnp.concatenate([x[mid:], x[:mid]], axis=0)  13.6 us
  transfers between devices with their start and end apart: 26, of which 8 were waited for; matrix products, arithmetic and copies ran while one was open for 31% of the time, Pallas kernels for 24%

profile of v1, /device:TPU:32, one launch (start us, length us, event | category | flops | bytes accessed | tf_op | source)
XLA Modules:
  0.0 424.5 jit_solution(3197981033250393367)
XLA Ops:
  7.3 11.1 %collective-permute-done.2 = f32[384]{0:T(512)S(1)} collective-permute-done((f32[384]{0:T(512)S(1)}, f32[384]{0:T(512)S(1)}, u32[]{:S(2)}, u32[]{:S(2)}) %collective-permute-start.2) | collective-permute-done | bytes 1568 | tf_op jit(solution)/shard_map/ppermute | solution.py:160
  22.0 9.6 %collective-permute-done = bf16[384,768]{1,0:T(8,128)(2,1)S(1)} collective-permute-done((bf16[384,768]{1,0:T(8,128)(2,1)S(1)}, bf16[384,768]{1,0:T(8,128)(2,1)S(1)}, u32[]{:S(2)}, u32[]{:S(2)}) %collective-permute-start) | collective-permute-done | bytes 589856 | tf_op jit(solution)/shard_map/ppermute | solution.py:160
  42.6 34.4 %inverse.3 = (f32[768,768]{1,0:T(8,128)S(1)}, f32[8,128]{1,0:T(8,128)S(1)}) custom-call(f32[768,768]{1,0:T(8,128)S(1)} %select_add_fusion.m_ref), custom_call_target="tpu_custom_call" | custom-call | flops 30000001024 | bytes 4718592 | tf_op jit(solution)/shard_map/inverse/pallas_call | solution.py:114
  77.5 3.3 collective-permute-start.24
  82.2 4.8 %fusion.123 = f32[768,384]{1,0:T(8,128)} fusion(f32[768,768]{1,0:T(8,128)S(1)} %get-tuple-element.9, f32[768,384]{0,1:T(8,128)S(1)} %fusion.78), kind=kOutput, calls=%fused_computation.199 | convolution fusion | flops 1358954496 | bytes 4718592 | tf_op jit(solution)/shard_map/dot_general | solution.py:131
  87.1 3.8 fusion.125
  98.4 3.5 fusion.16
  119.4 12.8 %collective-permute-done.13 = f32[768,384]{1,0:T(8,128)} collective-permute-done((f32[768,384]{1,0:T(8,128)}, f32[768,384]{1,0:T(8,128)}, u32[]{:S(2)}, u32[]{:S(2)}) %collective-permute-start.13) | collective-permute-done | bytes 1179680 | tf_op jit(solution)/shard_map/ppermute | solution.py:160
  138.5 3.3 fusion.17
  144.5 15.0 %collective-permute-done.11 = f32[768,416]{0,1:T(8,128)S(1)} collective-permute-done((f32[768,416]{0,1:T(8,128)}, f32[768,416]{0,1:T(8,128)S(1)}, u32[]{:S(2)}, u32[]{:S(2)}) %collective-permute-start.11) | collective-permute-done | bytes 1277984 | tf_op jit(solution)/shard_map/ppermute | solution.py:160
  166.5 3.3 copy.125
  172.6 34.4 %inverse.4 = (f32[768,768]{1,0:T(8,128)S(1)}, f32[8,128]{1,0:T(8,128)S(1)}) custom-call(f32[768,768]{1,0:T(8,128)S(1)} %maximum_maximum_fusion.m_ref), custom_call_target="tpu_custom_call" | custom-call | flops 30000001024 | bytes 4718592 | tf_op jit(solution)/shard_map/inverse/pallas_call | solution.py:114
  208.2 3.3 collective-permute-start.25
  220.8 3.3 fusion.114
  238.7 3.4 select_subtract_fusion.1
  243.8 4.4 %select_subtract_fusion = f32[768,384]{1,0:T(8,128)} fusion(f32[768,384]{1,0:T(8,128)} %fusion.17, f32[768,384]{1,0:T(8,128)} %collective-permute-done.9, pred[]{:T(512)S(6)} %ne.37, f32[768,384]{1,0:T(8,128)S(1)} %copy-done.22, f32[768,384]{1,0:T(8,128)S(1)} %get-tuple-element.29, f32[768,384]{1,0:T(8,128)S(1)} %get-tuple-element.43), kind=kOutput, calls=%fused_computation.71 | convolution fusion | flops 1360134144 | bytes 7077889 | tf_op jit(solution)/shard_map/dot_general | solution.py:131
  262.3 37.4 %collective-permute-done.16 = f32[768,384]{1,0:T(8,128)} collective-permute-done((f32[768,384]{1,0:T(8,128)}, f32[768,384]{1,0:T(8,128)}, u32[]{:S(2)}, u32[]{:S(2)}) %collective-permute-start.16) | collective-permute-done | bytes 1179680 | tf_op jit(solution)/shard_map/ppermute | solution.py:160
  306.1 19.5 %collective-permute-done.21 = f32[768,416]{0,1:T(8,128)S(1)} collective-permute-done((f32[768,416]{0,1:T(8,128)}, f32[768,416]{0,1:T(8,128)S(1)}, u32[]{:S(2)}, u32[]{:S(2)}) %collective-permute-start.21) | collective-permute-done | bytes 1277984 | tf_op jit(solution)/shard_map/ppermute | solution.py:160
  336.1 34.8 %inverse.5 = (f32[768,768]{1,0:T(8,128)S(1)}, f32[8,128]{1,0:T(8,128)S(1)}) custom-call(f32[768,768]{1,0:T(8,128)S(1)} %maximum_maximum_fusion.1.m_ref), custom_call_target="tpu_custom_call" | custom-call | flops 30000001024 | bytes 4718592 | tf_op jit(solution)/shard_map/inverse/pallas_call | solution.py:114
  387.3 4.6 %fusion.47 = f32[32,768]{0,1:T(8,128)S(1)} fusion(f32[768,32]{1,0:T(8,128)S(1)} %copy-done.35, f32[384,32]{1,0:T(8,128)} %get-tuple-element.71, f32[384,32]{1,0:T(8,128)} %get-tuple-element.72, pred[]{:T(512)S(6)} %eq.23, f32[768,32]{0,1:T(8,128)} %fusion.131, f32[768,384]{1,0:T(8,128)} %copy-done.7, f32[768,384]{1,0:T(8,128)} %get-tuple-element.28), kind=kOutput, calls=%fused_computation.108 | convolution fusion | flops 115089408 | bytes 2752513 | tf_op jit(solution)/shard_map/dot_general | solution.py:131
  392.7 5.2 %convolution_negate_fusion.1 = f32[384,768]{0,1:T(8,128)} fusion(f32[768,384]{1,0:T(8,128)} %fusion.129, f32[768,384]{1,0:T(8,128)S(1)} %copy-done.9, f32[768,384]{1,0:T(8,128)} %get-tuple-element.28, pred[]{:T(512)S(6)} %eq.23), kind=kOutput, calls=%fused_computation.47 | convolution fusion | flops 1361018880 | bytes 4718593 | tf_op jit(solution)/shard_map/dot_general | solution.py:131
  397.9 3.3 convolution_negate_fusion
  405.9 4.5 %fusion.29 = f32[384,768]{0,1:T(8,128)S(1)} fusion(f32[768,384]{1,0:T(8,128)S(1)} %copy-done.21, f32[384,384]{1,0:T(8,128)} %get-tuple-element.69, f32[384,384]{1,0:T(8,128)} %get-tuple-element.70, pred[]{:T(512)S(6)} %eq.23, f32[768,384]{1,0:T(8,128)} %fusion.130, f32[768,384]{1,0:T(8,128)S(1)} %copy-done.9, f32[768,384]{1,0:T(8,128)} %get-tuple-element.28), kind=kOutput, calls=%fused_computation.70 | convolution fusion | flops 1361608704 | bytes 7077889 | tf_op jit(solution)/shard_map/dot_general | solution.py:131
  416.4 6.1 %copy.156 = f32[1,2,384,1536]{3,2,1,0:T(8,128)} copy(f32[1,2,384,1536]{2,3,1,0:T(8,128)} %maximum_bitcast_fusion) | data formatting | bytes 9437184
  (270 shorter events, 149.2 us)
Async XLA Ops:
  2.0 31.3 %collective-permute-start.5 = (bf16[384,768]{1,0:T(8,128)(2,1)S(1)}, bf16[384,768]{1,0:T(8,128)(2,1)S(1)}, u32[]{:S(2)}, u32[]{:S(2)}) collective-permute-start(bf16[384,768]{1,0:T(8,128)(2,1)S(1)} %get-tuple-element.56), channel_id=1, source_target_pairs={{0,1},{1,0},{2,3},{3,2},{4,5},{5,4},{6,7},{7,6},{8,9},{9,8},{10,11... | collective-permute-start | bytes 1769480 | tf_op jit(solution)/shard_map/ppermute | solution.py:153
  2.1 18.5 %collective-permute-start.3 = (bf16[384,768]{1,0:T(8,128)(2,1)S(1)}, bf16[384,768]{1,0:T(8,128)(2,1)S(1)}, u32[]{:S(2)}, u32[]{:S(2)}) collective-permute-start(bf16[384,768]{1,0:T(8,128)(2,1)S(1)} %get-tuple-element.56), channel_id=1, source_target_pairs={{0,2},{2,0},{4,6},{6,4},{8,10},{10,8},{12,14},{14,12},{16,18},{18,... | collective-permute-start | bytes 1769480 | tf_op jit(solution)/shard_map/ppermute | solution.py:160
  3.7 14.7 %collective-permute-start.2 = (f32[384]{0:T(512)S(1)}, f32[384]{0:T(512)S(1)}, u32[]{:S(2)}, u32[]{:S(2)}) collective-permute-start(f32[384]{0:T(512)S(1)} %copy-done.66), channel_id=1, source_target_pairs={{0,2},{2,0},{4,6},{6,4},{8,10},{10,8},{12,14},{14,12},{16,18},{18,... | collective-permute-start | bytes 4616 | tf_op jit(solution)/shard_map/ppermute | solution.py:160
  4.2 15.2 %collective-permute-start.6 = (bf16[32,768]{1,0:T(8,128)(2,1)S(1)}, bf16[32,768]{1,0:T(8,128)(2,1)S(1)}, u32[]{:S(2)}, u32[]{:S(2)}) collective-permute-start(bf16[32,768]{1,0:T(8,128)(2,1)S(1)} %copy-done.63), channel_id=1, source_target_pairs={{0,2},{2,0},{4,6},{6,4},{8,10},{10,8},{12,14},{14,12},{16,18},{18,... | collective-permute-start | bytes 147464 | tf_op jit(solution)/shard_map/ppermute | solution.py:160
  5.7 25.9 %collective-permute-start = (bf16[384,768]{1,0:T(8,128)(2,1)S(1)}, bf16[384,768]{1,0:T(8,128)(2,1)S(1)}, u32[]{:S(2)}, u32[]{:S(2)}) collective-permute-start(bf16[384,768]{1,0:T(8,128)(2,1)S(1)} %get-tuple-element.55), channel_id=1, source_target_pairs={{0,2},{2,0},{4,6},{6,4},{8,10},{10,8},{12,14},{14,12},{16,18},{18,... | collective-permute-start | bytes 1769480 | tf_op jit(solution)/shard_map/ppermute | solution.py:160
  20.1 94.6 %collective-permute-start.18 = (bf16[32,768]{1,0:T(8,128)(2,1)}, bf16[32,768]{1,0:T(8,128)(2,1)}, u32[]{:S(2)}, u32[]{:S(2)}) collective-permute-start(bf16[32,768]{1,0:T(8,128)(2,1)} %get-tuple-element.63), channel_id=1, source_target_pairs={{0,1},{1,0},{2,3},{3,2},{4,5},{5,4},{6,7},{7,6},{8,9},{9,8},{10,11... | collective-permute-start | bytes 147464 | tf_op jit(solution)/shard_map/ppermute | solution.py:153
  20.7 12.6 %collective-permute-start.4 = (bf16[384,768]{1,0:T(8,128)(2,1)S(1)}, bf16[384,768]{1,0:T(8,128)(2,1)S(1)}, u32[]{:S(2)}, u32[]{:S(2)}) collective-permute-start(bf16[384,768]{1,0:T(8,128)(2,1)S(1)} %collective-permute-done.3), channel_id=1, source_target_pairs={{0,1},{1,0},{2,3},{3,2},{4,5},{5,4},{6,7},{7,6},{8,9},{9,8},{10,11... | collective-permute-start | bytes 1769480 | tf_op jit(solution)/shard_map/ppermute | solution.py:153
  32.7 65.6 %collective-permute-start.10 = (bf16[384,768]{1,0:T(8,128)(2,1)}, bf16[384,768]{1,0:T(8,128)(2,1)}, u32[]{:S(2)}, u32[]{:S(2)}) collective-permute-start(bf16[384,768]{1,0:T(8,128)(2,1)} %get-tuple-element.53), channel_id=1, source_target_pairs={{0,1},{1,0},{2,3},{3,2},{4,5},{5,4},{6,7},{7,6},{8,9},{9,8},{10,11... | collective-permute-start | bytes 1769480 | tf_op jit(solution)/shard_map/ppermute | solution.py:153
  32.7 85.0 %collective-permute-start.1 = (bf16[384,768]{1,0:T(8,128)(2,1)}, bf16[384,768]{1,0:T(8,128)(2,1)}, u32[]{:S(2)}, u32[]{:S(2)}) collective-permute-start(bf16[384,768]{1,0:T(8,128)(2,1)} %get-tuple-element.54), channel_id=1, source_target_pairs={{0,1},{1,0},{2,3},{3,2},{4,5},{5,4},{6,7},{7,6},{8,9},{9,8},{10,11... | collective-permute-start | bytes 1769480 | tf_op jit(solution)/shard_map/ppermute | solution.py:153
  40.3 51.9 %collective-permute-start.7 = (f32[768,800]{0,1:T(8,128)}, f32[768,800]{0,1:T(8,128)}, u32[]{:S(2)}, u32[]{:S(2)}) collective-permute-start(f32[768,800]{0,1:T(8,128)} %pad_maximum_fusion.2), channel_id=1, source_target_pairs={{0,1},{1,0},{2,3},{3,2},{4,5},{5,4},{6,7},{7,6},{8,9},{9,8},{10,11... | collective-permute-start | bytes 7372808 | tf_op jit(solution)/shard_map/ppermute | solution.py:153
  77.5 13.4 %collective-permute-start.24 = (f32[]{:T(128)}, f32[]{:T(128)}, u32[]{:S(2)}, u32[]{:S(2)}) collective-permute-start(f32[]{:T(128)} %bitcast.9), channel_id=1, source_target_pairs={{0,6},{2,4},{4,2},{6,0},{8,14},{10,12},{12,10},{14,8},{16,22},{18,... | collective-permute-start | bytes 20 | tf_op jit(solution)/shard_map/ppermute | solution.py:160
  101.9 30.3 %collective-permute-start.13 = (f32[768,384]{1,0:T(8,128)}, f32[768,384]{1,0:T(8,128)}, u32[]{:S(2)}, u32[]{:S(2)}) collective-permute-start(f32[768,384]{1,0:T(8,128)} %fusion.16), channel_id=1, source_target_pairs={{0,6},{2,4},{4,2},{6,0},{8,14},{10,12},{12,10},{14,8},{16,22},{18,... | collective-permute-start | bytes 3538952 | tf_op jit(solution)/shard_map/ppermute | solution.py:160
  111.9 47.6 %collective-permute-start.11 = (f32[768,416]{0,1:T(8,128)}, f32[768,416]{0,1:T(8,128)S(1)}, u32[]{:S(2)}, u32[]{:S(2)}) collective-permute-start(f32[768,416]{0,1:T(8,128)} %copy.122), channel_id=1, source_target_pairs={{0,6},{2,4},{4,2},{6,0},{8,14},{10,12},{12,10},{14,8},{16,22},{18,... | collective-permute-start | bytes 3833864 | tf_op jit(solution)/shard_map/ppermute | solution.py:160
  135.2 34.6 %collective-permute-start.14 = (f32[768,384]{1,0:T(8,128)}, f32[768,384]{1,0:T(8,128)}, u32[]{:S(2)}, u32[]{:S(2)}) collective-permute-start(f32[768,384]{1,0:T(8,128)} %add.66), channel_id=1, source_target_pairs={{0,1},{1,0},{2,3},{3,2},{4,5},{5,4},{6,7},{7,6},{8,9},{9,8},{10,11... | collective-permute-start | bytes 3538952 | tf_op jit(solution)/shard_map/ppermute | solution.py:153
  136.0 94.2 %collective-permute-start.20 = (f32[832,32]{1,0:T(8,128)}, f32[832,32]{1,0:T(8,128)}, u32[]{:S(2)}, u32[]{:S(2)}) collective-permute-start(f32[832,32]{1,0:T(8,128)} %pad_maximum_fusion.30), channel_id=1, source_target_pairs={{0,6},{2,4},{4,2},{6,0},{8,14},{10,12},{12,10},{14,8},{16,22},{18,... | collective-permute-start | bytes 319496 | tf_op jit(solution)/shard_map/ppermute | solution.py:160
  141.8 96.9 %collective-permute-start.9 = (f32[768,384]{1,0:T(8,128)}, f32[768,384]{1,0:T(8,128)}, u32[]{:S(2)}, u32[]{:S(2)}) collective-permute-start(f32[768,384]{1,0:T(8,128)} %fusion.17), channel_id=1, source_target_pairs={{0,6},{2,4},{4,2},{6,0},{8,14},{10,12},{12,10},{14,8},{16,22},{18,... | collective-permute-start | bytes 3538952 | tf_op jit(solution)/shard_map/ppermute | solution.py:160
  169.8 51.0 %collective-permute-start.12 = (f32[768,800]{0,1:T(8,128)}, f32[768,800]{0,1:T(8,128)}, u32[]{:S(2)}, u32[]{:S(2)}) collective-permute-start(f32[768,800]{0,1:T(8,128)} %copy.125), channel_id=1, source_target_pairs={{0,1},{1,0},{2,3},{3,2},{4,5},{5,4},{6,7},{7,6},{8,9},{9,8},{10,11... | collective-permute-start | bytes 7372808 | tf_op jit(solution)/shard_map/ppermute | solution.py:153
  208.2 12.0 %collective-permute-start.25 = (f32[]{:T(128)}, f32[]{:T(128)}, u32[]{:S(2)}, u32[]{:S(2)}) collective-permute-start(f32[]{:T(128)} %add.73), channel_id=1, source_target_pairs={{0,8},{2,10},{4,12},{6,14},{8,0},{10,2},{12,4},{14,6},{16,24},{18,... | collective-permute-start | bytes 20 | tf_op jit(solution)/shard_map/ppermute | solution.py:160
  236.0 22.3 %collective-permute-start.23 = (f32[832,32]{1,0:T(8,128)}, f32[832,32]{1,0:T(8,128)}, u32[]{:S(2)}, u32[]{:S(2)}) collective-permute-start(f32[832,32]{1,0:T(8,128)} %pad_maximum_fusion.31), channel_id=1, source_target_pairs={{0,8},{2,10},{4,12},{6,14},{8,0},{10,2},{12,4},{14,6},{16,24},{18,... | collective-permute-start | bytes 319496 | tf_op jit(solution)/shard_map/ppermute | solution.py:160
  242.1 60.4 %collective-permute-start.15 = (f32[768,384]{1,0:T(8,128)S(1)}, f32[768,384]{1,0:T(8,128)}, u32[]{:S(2)}, u32[]{:S(2)}) collective-permute-start(f32[768,384]{1,0:T(8,128)S(1)} %select_subtract_fusion.1), channel_id=1, source_target_pairs={{0,8},{2,10},{4,12},{6,14},{8,0},{10,2},{12,4},{14,6},{16,24},{18,... | collective-permute-start | bytes 3538952 | tf_op jit(solution)/shard_map/ppermute | solution.py:160
  248.1 51.6 %collective-permute-start.16 = (f32[768,384]{1,0:T(8,128)}, f32[768,384]{1,0:T(8,128)}, u32[]{:S(2)}, u32[]{:S(2)}) collective-permute-start(f32[768,384]{1,0:T(8,128)} %select_subtract_fusion), channel_id=1, source_target_pairs={{0,8},{2,10},{4,12},{6,14},{8,0},{10,2},{12,4},{14,6},{16,24},{18,... | collective-permute-start | bytes 3538952 | tf_op jit(solution)/shard_map/ppermute | solution.py:160
  256.7 68.9 %collective-permute-start.21 = (f32[768,416]{0,1:T(8,128)}, f32[768,416]{0,1:T(8,128)S(1)}, u32[]{:S(2)}, u32[]{:S(2)}) collective-permute-start(f32[768,416]{0,1:T(8,128)} %copy.138), channel_id=1, source_target_pairs={{0,8},{2,10},{4,12},{6,14},{8,0},{10,2},{12,4},{14,6},{16,24},{18,... | collective-permute-start | bytes 3833864 | tf_op jit(solution)/shard_map/ppermute | solution.py:160
  302.5 30.8 %collective-permute-start.17 = (f32[768,384]{1,0:T(8,128)}, f32[768,384]{1,0:T(8,128)}, u32[]{:S(2)}, u32[]{:S(2)}) collective-permute-start(f32[768,384]{1,0:T(8,128)} %add.67), channel_id=1, source_target_pairs={{0,1},{1,0},{2,3},{3,2},{4,5},{5,4},{6,7},{7,6},{8,9},{9,8},{10,11... | collective-permute-start | bytes 3538952 | tf_op jit(solution)/shard_map/ppermute | solution.py:153
  333.1 46.7 %collective-permute-start.22 = (f32[768,800]{0,1:T(8,128)}, f32[768,800]{0,1:T(8,128)}, u32[]{:S(2)}, u32[]{:S(2)}) collective-permute-start(f32[768,800]{0,1:T(8,128)} %copy.141), channel_id=1, source_target_pairs={{0,1},{1,0},{2,3},{3,2},{4,5},{5,4},{6,7},{7,6},{8,9},{9,8},{10,11... | collective-permute-start | bytes 7372808 | tf_op jit(solution)/shard_map/ppermute | solution.py:153
  (70 other events, 356.0 us)
